TPU v7x, 128 devices: a whole 4x4x4 slice. The times are simulated.
128 devices in a mesh: dp: 32 (over x_hi, y, z), feat: 4 (over x_lo, core).
Axes of the slice: x: 4 (x_hi: 2, x_lo: 2; x = x_hi * 2 + x_lo), y: 4, z: 4, core: 2. Of those that a mesh axis runs over, the one named last changes fastest.
Arguments:
- view_a: bfloat16 [24576, 4096], P('dp', 'feat'), may hold values from -4000 to 4000, as said below
- view_b: bfloat16 [24576, 4096], P('dp', 'feat'), may hold values from -4000 to 4000, as said below
Outputs:
- loss: float32 [], replicated
- grad_a: bfloat16 [24576, 4096], P('dp', 'feat')
- grad_b: bfloat16 [24576, 4096], P('dp', 'feat')
Inputs may be any that keep to these rules, and one draw needn't show every extreme that they name: `view_a`: for every feature, the magnitude of its mean over all 24576 samples is at most 20 times its standard deviation over them, and that standard deviation is 0.5 or more. `view_b`: for every feature, the magnitude of its mean over all 24576 samples is at most 20 times its standard deviation over them, and that standard deviation is 0.5 or more.
All inputs are finite; a program needn't handle non-finite values.
Results may differ from a plain program's by a relative error of at most 0.0039.
Values may be sent and summed in bfloat16 or wider, within the bound.
No kernel may reach another device: no remote copies, remote signals or barrier semaphores. Data moves between devices by JAX's collectives and lax.ppermute only.
A program may use at most 128 MiB of HBM per device.

v0:
```python
import jax
import jax.numpy as jnp
from jax import lax
from jax.sharding import PartitionSpec as P

epsilon = 1e-05
off_weight = 0.0051


def backward(upstream, normed, inverse, sum_up, sum_cross, pairs):
    return (inverse * (upstream - sum_up / pairs - normed * (sum_cross / pairs))).astype(
        jnp.bfloat16
    )


def on_device(view_a, view_b):
    dp_count = lax.axis_size("dp")
    feat_count = lax.axis_size("feat")
    rows, width = view_a.shape
    pairs = rows * dp_count
    full_width = width * feat_count
    first = view_a.astype(jnp.float32)
    second = view_b.astype(jnp.float32)
    sum_first, sum_second = lax.psum((jnp.sum(first, axis=0), jnp.sum(second, axis=0)), "dp")
    centred_a = first - sum_first / pairs
    centred_b = second - sum_second / pairs
    square_a, square_b = lax.psum(
        (jnp.sum(centred_a * centred_a, axis=0), jnp.sum(centred_b * centred_b, axis=0)), "dp"
    )
    var_a = square_a / pairs
    var_b = square_b / pairs
    inv_a = lax.rsqrt(var_a + epsilon)
    inv_b = lax.rsqrt(var_b + epsilon)
    norm_a = centred_a * inv_a
    norm_b = centred_b * inv_b
    low_a = norm_a.astype(jnp.bfloat16)
    low_b = norm_b.astype(jnp.bfloat16)
    second_full = lax.all_gather(low_b, "feat", axis=1, tiled=True)
    dp_index = lax.axis_index("dp")
    feat_index = lax.axis_index("feat")
    keep = width // dp_count
    row_ids = feat_index * width + dp_index * keep + jnp.arange(keep, dtype=jnp.int32)
    col_ids = jnp.arange(full_width, dtype=jnp.int32)
    corr_tile = (
        lax.psum_scatter(
            lax.dot_general(
                low_a, second_full, (((0,), (0,)), ((), ())), preferred_element_type=jnp.float32
            ),
            "dp",
            scatter_dimension=0,
            tiled=True,
        )
        / pairs
    )
    on_diagonal = row_ids[:, None] == col_ids[None, :]
    partial_value = jnp.sum(
        jnp.where(
            on_diagonal, (1.0 - corr_tile) * (1.0 - corr_tile), off_weight * corr_tile * corr_tile
        )
    )
    loss = lax.psum(partial_value, ("dp", "feat"))
    slope = jnp.where(on_diagonal, -2.0 * (1.0 - corr_tile), 2.0 * off_weight * corr_tile).astype(
        jnp.bfloat16
    )
    gathered = lax.all_gather(slope, "dp", axis=0, tiled=True)
    up_a = lax.dot_general(
        second_full, gathered, (((1,), (1,)), ((), ())), preferred_element_type=jnp.float32
    )
    part_b = jnp.dot(low_a, gathered, preferred_element_type=jnp.float32)
    up_b = lax.psum_scatter(part_b, "feat", scatter_dimension=1, tiled=True)
    sum_up_a, cross_a, sum_up_b, cross_b = lax.psum(
        (
            jnp.sum(up_a, axis=0),
            jnp.sum(up_a * norm_a, axis=0),
            jnp.sum(up_b, axis=0),
            jnp.sum(up_b * norm_b, axis=0),
        ),
        "dp",
    )
    grad_a = backward(up_a, norm_a, inv_a, sum_up_a, cross_a, pairs)
    grad_b = backward(up_b, norm_b, inv_b, sum_up_b, cross_b, pairs)
    return (loss, grad_a, grad_b)


def solution(mesh):
    in_specs = (P("dp", "feat"), P("dp", "feat"))
    out_specs = (P(), P("dp", "feat"), P("dp", "feat"))
    return jax.shard_map(
        on_device, mesh=mesh, in_specs=in_specs, out_specs=out_specs, check_vma=False
    )
```

profile of v0, /device:TPU:0, one launch (start us, length us, event | category | flops | bytes accessed | tf_op | source)
XLA Modules:
  0.0 929.1 jit_solution(3711676328444292066)
XLA Ops:
  7.2 0.0 all-gather.3.cloned.1.call-start
  7.2 1.8 convert_reduce_fusion
  9.1 1.7 convert_reduce_fusion.1
  10.7 99.0 %all-reduce.2 = (f32[1024]{0:T(1024)S(1)}, f32[1024]{0:T(1024)S(1)}) all-reduce(f32[1024]{0:T(1024)S(1)} %convert_reduce_fusion, f32[1024]{0:T(1024)S(1)} %convert_reduce_fusion.1), channel_id=1, replica_groups=mesh['dp'=32,'feat'=4] {'dp'}, use_global_device_ids=true, to_apply=%region_5.0 | all-reduce | flops 2048 | bytes 16384 | tf_op jit(solution)/shard_map/psum | solution.py:24
  109.8 0.5 fusion.14
  110.3 0.5 fusion.19
  110.7 89.9 %all-reduce.1 = (f32[1024]{0:T(1024)S(1)}, f32[1024]{0:T(1024)S(1)}) all-reduce(f32[1024]{0:T(1024)S(1)} %fusion.14, f32[1024]{0:T(1024)S(1)} %fusion.19), channel_id=1, replica_groups=mesh['dp'=32,'feat'=4] {'dp'}, use_global_device_ids=true, to_apply=%region_7.0 | all-reduce | flops 2048 | bytes 16384 | tf_op jit(solution)/shard_map/psum | solution.py:27
  200.7 1.6 fusion.9
  202.3 0.0 reduce-scatter.3.cloned.1.call-start
  202.3 58.9 %all-gather.3.cloned.1.call-done = bf16[768,4096]{1,0:T(8,128)(2,1)} async-done(((bf16[768,1024]{1,0:T(8,128)(2,1)}), bf16[768,4096]{1,0:T(8,128)(2,1)}) %all-gather.3.cloned.1.call-update) | async-done | bytes 6291472 | tf_op jit(solution)/shard_map/all_gather | solution.py:38
  261.3 13.0 %fusion.22 = f32[1024,4096]{1,0:T(8,128)} fusion(bf16[768,4096]{1,0:T(8,128)(2,1)} %all-gather.3.cloned.1.call-done, bf16[768,1024]{1,0:T(8,128)(2,1)S(1)} %copy-done.1, f32[1024]{0:T(1024)S(1)} %add_rsqrt_fusion.1, f32[1024]{0:T(1024)S(1)} %get-tuple-element.19), kind=kOutput, calls=%fused_computation.25 | convolution fusion | flops 6445596672 | bytes 24649728 | tf_op jit(solution)/shard_map/dot_general | solution.py:46
  274.3 0.0 all-gather.5.cloned.1.call-start
  274.4 227.4 %reduce-scatter.3.cloned.1.call-done = f32[32,4096]{1,0:T(8,128)} async-done(((f32[1024,4096]{1,0:T(8,128)}), f32[32,4096]{1,0:T(8,128)}) %reduce-scatter.3.cloned.1.call-update) | async-done | bytes 524304 | tf_op jit(solution)/shard_map/reduce_scatter | solution.py:45
  501.8 2.6 select_convert_fusion
  504.4 0.0 reduce-scatter.5.cloned.1.call-start
  504.4 101.7 %all-gather.5.cloned.1.call-done = bf16[1024,4096]{1,0:T(8,128)(2,1)} async-done(((bf16[32,4096]{1,0:T(8,128)(2,1)}), bf16[1024,4096]{1,0:T(8,128)(2,1)}) %all-gather.5.cloned.1.call-update) | async-done | bytes 8388624 | tf_op jit(solution)/shard_map/all_gather | solution.py:65
  606.1 12.4 %fusion.20 = f32[768,4096]{1,0:T(8,128)} fusion(bf16[1024,4096]{1,0:T(8,128)(2,1)} %all-gather.5.cloned.1.call-done, bf16[768,1024]{1,0:T(8,128)(2,1)S(1)} %copy-done.1, f32[1024]{0:T(1024)S(1)} %add_rsqrt_fusion.1, f32[1024]{0:T(1024)S(1)} %get-tuple-element.19), kind=kOutput, calls=%fused_computation.24 | convolution fusion | flops 6445596672 | bytes 22552576 | tf_op jit(solution)/shard_map/dot_general | solution.py:69
  618.5 64.7 %psum.67 = f32[]{:T(128)} all-reduce(f32[]{:T(128)} %get-tuple-element.16), channel_id=1, replica_groups=mesh['dp'=32,'feat'=4] {'dp','feat'}, use_global_device_ids=true, to_apply=%region_10.11 | all-reduce | flops 1 | bytes 8 | tf_op jit(solution)/shard_map/psum | solution.py:61
  683.2 12.4 %fusion.25 = (f32[1024]{0:T(1024)S(1)}, f32[1024]{0:T(1024)S(1)}, f32[768,1024]{1,0:T(8,128)}) fusion(f32[1024]{0:T(1024)S(1)} %add_rsqrt_fusion.1, f32[1024]{0:T(1024)S(1)} %get-tuple-element.19, bf16[768,1024]{1,0:T(8,128)(2,1)S(1)} %copy-done.1, bf16[768,4096]{1,0:T(8,128)(2,1)} %all-gather.3.cloned.1.call-done, ...), kind=kOutput, calls=%fused_computation.39 | convolution fusion | flops 6447167488 | bytes 19415040 | tf_op jit(solution)/shard_map/dot_general | solution.py:66
  695.6 35.4 %reduce-scatter.5.cloned.1.call-done = f32[768,1024]{1,0:T(8,128)} async-done(((f32[768,4096]{1,0:T(8,128)}), f32[768,1024]{1,0:T(8,128)}) %reduce-scatter.5.cloned.1.call-update) | async-done | bytes 3145744 | tf_op jit(solution)/shard_map/reduce_scatter | solution.py:70
  730.9 2.6 fusion.24
  733.5 183.1 %all-reduce = (f32[1024]{0:T(1024)S(1)}, f32[1024]{0:T(1024)S(1)}, f32[1024]{0:T(1024)S(1)}, f32[1024]{0:T(1024)S(1)}) all-reduce(f32[1024]{0:T(1024)S(1)} %get-tuple-element.6, f32[1024]{0:T(1024)S(1)} %get-tuple-element.5, f32[1024]{0:T(1024)S(1)} %get-tuple-element.4, ...), channel_id=1, replica_groups=mesh['dp'=32,'feat'=4] {'dp'}, use_global_device_ids=true, to_apply=%region_14.15 | all-reduce | flops 4096 | bytes 32768 | tf_op jit(solution)/shard_map/psum | solution.py:71
  916.6 4.0 fusion.18
  920.6 1.9 fusion.13
  (18 shorter events, 0.1 us)
Async XLA Ops:
  7.2 102.6 %copy-start = (bf16[768,1024]{1,0:T(8,128)(2,1)S(1)}, bf16[768,1024]{1,0:T(8,128)(2,1)}, u32[]{:S(2)}) copy-start(bf16[768,1024]{1,0:T(8,128)(2,1)} %param.3) | copy-start | bytes 4718596
  7.2 103.1 %copy-start.1 = (bf16[768,1024]{1,0:T(8,128)(2,1)S(1)}, bf16[768,1024]{1,0:T(8,128)(2,1)}, u32[]{:S(2)}) copy-start(bf16[768,1024]{1,0:T(8,128)(2,1)} %param.2) | copy-start | bytes 4718596
  7.2 254.1 %all-gather.3.cloned.1.call-start = ((), (), s32[]{:S(2)}) async-start(), calls=%async_computation.2 | async-start | bytes 7864320 | tf_op jit(solution)/shard_map/all_gather | solution.py:38
  202.3 299.5 %reduce-scatter.3.cloned.1.call-start = ((), (), s32[]{:S(2)}) async-start(), calls=%async_computation.3 | async-start | bytes 17301504 | tf_op jit(solution)/shard_map/reduce_scatter | solution.py:45
  274.3 331.8 %all-gather.5.cloned.1.call-start = ((), (), s32[]{:S(2)}) async-start(), calls=%async_computation.4 | async-start | bytes 8650752 | tf_op jit(solution)/shard_map/all_gather | solution.py:65
  504.4 226.5 %reduce-scatter.5.cloned.1.call-start = ((), (), s32[]{:S(2)}) async-start(), calls=%async_computation.5 | async-start | bytes 15728640 | tf_op jit(solution)/shard_map/reduce_scatter | solution.py:70
  916.6 4.0 copy-start.2
Sparse Core Ops, SparseCore 0:
  202.4 58.8 all-gather.2
  274.4 227.2 reduce-scatter.2
  505.5 100.5 all-gather.4
  618.6 112.2 reduce-scatter.4
where the time goes:
time: 929 us
  blocking collectives  437 us (47%)
  waiting for transfers between devices  423 us (46%)
  matrix products  37.8 us (4%)
  other arithmetic  17.1 us (2%)
  between operations  13.9 us (1%)
    reduce_scatter x1, waiting for transfers between devices, on_device(): lax.psum_scatter(lax.dot_general(low_a, second_full, (((0,), (0,)), ((),...  227 us
    psum x1, blocking collectives, on_device(): lax.psum((jnp.sum(up_a, axis=0), jnp.sum(up_a * norm_a, axis=0), jnp.sum(...  183 us
    all_gather x1, waiting for transfers between devices, on_device(): gathered = lax.all_gather(slope, 'dp', axis=0, tiled=True)  102 us
    psum x1, blocking collectives, on_device(): lax.psum((jnp.sum(first, axis=0), jnp.sum(second, axis=0)), 'dp')  99 us
    psum x1, blocking collectives, on_device(): lax.psum((jnp.sum(centred_a * centred_a, axis=0), jnp.sum(centred_b * cen...  89.9 us
    psum x1, blocking collectives, on_device(): loss = lax.psum(partial_value, ('dp', 'feat'))  64.7 us
    all_gather x1, waiting for transfers between devices, on_device(): second_full = lax.all_gather(low_b, 'feat', axis=1, tiled=True)  58.9 us
    reduce_scatter x1, waiting for transfers between devices, on_device(): up_b = lax.psum_scatter(part_b, 'feat', scatter_dimension=1, tiled=True)  35.4 us
  transfers between devices with their start and end apart: 4, of which 4 were waited for; matrix products, arithmetic and copies ran while one was open for 1% of the time, Pallas kernels for 0%

commit v1 on v0

v1 whole, which is shorter than its diff:
```python
import jax
import jax.numpy as jnp
from jax import lax
from jax.sharding import PartitionSpec as P

epsilon = 1e-05
off_weight = 0.0051


def exchange(pieces):
    return lax.all_to_all(pieces, "dp", 0, 0, tiled=True)


def share(values):
    count = lax.axis_size("dp")
    return exchange(jnp.broadcast_to(values[None], (count,) + values.shape))


def local_moments(values):
    mean = jnp.mean(values, axis=0)
    centred = values - mean
    return mean, jnp.sum(centred * centred, axis=0)


def combine(means, squares, pairs):
    count = means.shape[0]
    mean = jnp.mean(means, axis=0)
    shift = means - mean
    var = (jnp.sum(squares, axis=0) + (pairs // count) * jnp.sum(shift * shift, axis=0)) / pairs
    return mean, lax.rsqrt(var + epsilon)


def backward(upstream, normed, inverse, sum_up, sum_cross, pairs):
    return (inverse * (upstream - sum_up / pairs - normed * (sum_cross / pairs))).astype(
        jnp.bfloat16
    )


def on_device(view_a, view_b):
    dp_count = lax.axis_size("dp")
    feat_count = lax.axis_size("feat")
    rows, width = view_a.shape
    pairs = rows * dp_count
    full_width = width * feat_count
    first = view_a.astype(jnp.float32)
    second = view_b.astype(jnp.float32)
    moments = jnp.stack(local_moments(first) + local_moments(second))
    shared = share(moments.reshape(-1, 128)).reshape(dp_count, 4, width)
    mean_a, inv_a = combine(shared[:, 0], shared[:, 1], pairs)
    mean_b, inv_b = combine(shared[:, 2], shared[:, 3], pairs)
    norm_a = (first - mean_a) * inv_a
    norm_b = (second - mean_b) * inv_b
    low_a = norm_a.astype(jnp.bfloat16)
    low_b = norm_b.astype(jnp.bfloat16)
    second_full = lax.all_gather(low_b, "feat", axis=1, tiled=True)
    dp_index = lax.axis_index("dp")
    feat_index = lax.axis_index("feat")
    keep = width // dp_count
    row_ids = feat_index * width + dp_index * keep + jnp.arange(keep, dtype=jnp.int32)
    col_ids = jnp.arange(full_width, dtype=jnp.int32)
    diagonal = jnp.sum(low_a.astype(jnp.float32) * low_b.astype(jnp.float32), axis=0)
    diagonal = jnp.sum(share(diagonal.reshape(-1, 128)), axis=0).reshape(dp_count, keep)
    diagonal = lax.dynamic_index_in_dim(diagonal, dp_index, 0, keepdims=False)
    part = lax.dot_general(
        low_a, second_full, (((0,), (0,)), ((), ())), preferred_element_type=jnp.float32
    ).astype(jnp.bfloat16)
    tiles = exchange(part.reshape(dp_count, keep, full_width))
    tile = jnp.sum(tiles.astype(jnp.float32), axis=0)
    on_diagonal = row_ids[:, None] == col_ids[None, :]
    corr_tile = jnp.where(on_diagonal, diagonal[:, None], tile) / pairs
    partial_value = jnp.sum(
        jnp.where(
            on_diagonal, (1.0 - corr_tile) * (1.0 - corr_tile), off_weight * corr_tile * corr_tile
        )
    )
    slope = jnp.where(on_diagonal, -2.0 * (1.0 - corr_tile), 2.0 * off_weight * corr_tile).astype(
        jnp.bfloat16
    )
    gathered = share(slope).reshape(width, full_width)
    part_b = jnp.dot(low_a, gathered, preferred_element_type=jnp.float32)
    up_b = lax.psum_scatter(
        part_b.astype(jnp.bfloat16), "feat", scatter_dimension=1, tiled=True
    ).astype(jnp.float32)
    up_a = lax.dot_general(
        second_full, gathered, (((1,), (1,)), ((), ())), preferred_element_type=jnp.float32
    )
    sums = jnp.stack(
        (
            jnp.sum(up_a, axis=0),
            jnp.sum(up_a * norm_a, axis=0),
            jnp.sum(up_b, axis=0),
            jnp.sum(up_b * norm_b, axis=0),
            jnp.full((width,), partial_value),
        )
    )
    sums = jnp.sum(share(sums.reshape(-1, 128)), axis=0).reshape(5, width)
    loss = jnp.sum(lax.all_gather(sums[4, :128], "feat")[:, 0])
    grad_a = backward(up_a, norm_a, inv_a, sums[0], sums[1], pairs)
    grad_b = backward(up_b, norm_b, inv_b, sums[2], sums[3], pairs)
    return (loss, grad_a, grad_b)


def solution(mesh):
    in_specs = (P("dp", "feat"), P("dp", "feat"))
    out_specs = (P(), P("dp", "feat"), P("dp", "feat"))
    return jax.shard_map(
        on_device, mesh=mesh, in_specs=in_specs, out_specs=out_specs, check_vma=False
    )
```

time: 929 us -> 489 us (0.53)
  blocking collectives: 437 us -> 159 us
  waiting for transfers between devices: 423 us -> 235 us
  starting transfers between devices: 0.16 us -> 13.8 us
    psum x4 -> x0, blocking collectives: 437 us -> none  [the longest x1 183 us: on_device(): lax.psum((jnp.sum(up_a, axis=0), jnp.sum(up_a * norm_a, axis=0), jnp.sum(...]
    reduce_scatter x2 -> x1, waiting for transfers between devices: 263 us -> 46.9 us  [on_device(): lax.psum_scatter(part_b.astype(jnp.bfloat16), 'feat', scatter_dimension=1...]
    all_to_all x0 -> x3, blocking collectives: none -> 154 us  [exchange(): return lax.all_to_all(pieces, 'dp', 0, 0, tiled=True)]
    all_to_all x0 -> x2, waiting for transfers between devices: none -> 134 us  [exchange(): return lax.all_to_all(pieces, 'dp', 0, 0, tiled=True)]
    all_gather x1 -> x0, waiting for transfers between devices: 102 us -> none  [on_device(): gathered = lax.all_gather(slope, 'dp', axis=0, tiled=True)]
    all_to_all x0 -> x2, starting transfers between devices: none -> 13.7 us  [exchange(): return lax.all_to_all(pieces, 'dp', 0, 0, tiled=True)]
    reduce_sum x5 -> x12, other arithmetic: 6.99 us -> 16.5 us  [the longest x1 5.23 us: on_device(): tile = jnp.sum(tiles.astype(jnp.float32), axis=0)]
  transfers between devices with their start and end apart: 4 -> 4, of which waited for: 4 -> 3; matrix products, arithmetic and copies ran while one was open for 1% -> 5% of each run, Pallas kernels for 0% -> 0%
where the time goes in v1:
time: 489 us; the launch traced here: 487 us
  waiting for transfers between devices  235 us (48%)
  blocking collectives  159 us (33%)
  matrix products  32.8 us (7%)
  other arithmetic  25 us (5%)
  between operations  14.2 us (3%)
  starting transfers between devices  13.8 us (3%)
  local copies, waits for them, and re-layouts  7.91 us (2%)
    all_to_all x3, blocking collectives, exchange(): return lax.all_to_all(pieces, 'dp', 0, 0, tiled=True)  154 us
    all_to_all x2, waiting for transfers between devices, exchange(): return lax.all_to_all(pieces, 'dp', 0, 0, tiled=True)  134 us
    all_gather x1, waiting for transfers between devices, on_device(): second_full = lax.all_gather(low_b, 'feat', axis=1, tiled=True)  54.1 us
    reduce_scatter x1, waiting for transfers between devices, on_device(): lax.psum_scatter(part_b.astype(jnp.bfloat16), 'feat', scatter_dimension=1...  46.9 us
    all_to_all x2, starting transfers between devices, exchange(): return lax.all_to_all(pieces, 'dp', 0, 0, tiled=True)  13.7 us
    dot_general x1, matrix products, on_device(): lax.dot_general(second_full, gathered, (((1,), (1,)), ((), ())), preferre...  12.4 us
    dot_general x1, matrix products, on_device(): lax.dot_general(low_a, second_full, (((0,), (0,)), ((), ())), preferred_e...  11.8 us
  transfers between devices with their start and end apart: 4, of which 3 were waited for; matrix products, arithmetic and copies ran while one was open for 5% of the time, Pallas kernels for 0%

profile of v1, /device:TPU:0, one launch (start us, length us, event | category | flops | bytes accessed | tf_op | source)
XLA Modules:
  0.0 487.4 jit_solution(10384458406293970783)
XLA Ops:
  7.2 1.8 convert_reduce_fusion.3
  9.0 1.9 fusion.1
  11.7 23.8 %all_to_all.25 = f32[32,32,128]{2,1,0:T(8,128)} all-to-all(f32[32,32,128]{2,1,0:T(8,128)S(1)} %broadcast_in_dim.25), channel_id=1, replica_groups=mesh['dp'=32,'feat'=4] {'dp'}, dimensions={0} | all-to-all | bytes 1048576 | tf_op jit(solution)/shard_map/all_to_all | solution.py:11
  35.5 2.0 reshape.148
  37.5 2.5 fusion.31
  40.1 2.0 multiply_reduce_fusion
  42.8 4.2 all-to-all-start.1
  47.0 54.1 %all-gather.3.cloned.1.call-done = bf16[768,4096]{1,0:T(8,128)(2,1)} async-done(((bf16[768,1024]{1,0:T(8,128)(2,1)}), bf16[768,4096]{1,0:T(8,128)(2,1)}) %all-gather.3.cloned.1.call-update) | async-done | bytes 6291472 | tf_op jit(solution)/shard_map/all_gather | solution.py:55
  101.2 11.8 %convolution_convert_fusion = bf16[1024,4096]{1,0:T(8,128)(2,1)} fusion(bf16[768,4096]{1,0:T(8,128)(2,1)} %all-gather.3.cloned.1.call-done, bf16[768,1024]{1,0:T(8,128)(2,1)S(1)} %copy-done.1, f32[1024]{0:T(1024)S(1)} %add_rsqrt_fusion, f32[1024]{0:T(1024)S(1)} %broadcast_multiply_fusion), kind=kOutput, calls=%fused_computation.1 | convolution fusion | flops 6449790976 | bytes 16261120 | tf_op jit(solution)/shard_map/dot_general | solution.py:64
  113.0 9.5 %all-to-all-start.2 = ((bf16[32,32,4096]{2,1,0:T(8,128)(2,1)}), bf16[32,32,4096]{2,1,0:T(8,128)(2,1)}, u32[]{:S(2)}, u32[]{:S(2)}) async-start(bf16[32,32,4096]{2,1,0:T(8,128)(2,1)} %bitcast.40), calls=%async_computation.2 | async-start | bytes 16777216 | tf_op jit(solution)/shard_map/all_to_all | solution.py:11
  122.7 133.5 %all-to-all-done.2 = bf16[32,32,4096]{2,1,0:T(8,128)(2,1)} async-done(((bf16[32,32,4096]{2,1,0:T(8,128)(2,1)}), bf16[32,32,4096]{2,1,0:T(8,128)(2,1)}, u32[]{:S(2)}, u32[]{:S(2)}) %all-to-all-start.2) | async-done | bytes 8388640 | tf_op jit(solution)/shard_map/all_to_all | solution.py:11
  256.3 5.2 %convert_reduce_fusion = f32[32,4096]{1,0:T(8,128)S(1)} fusion(bf16[32,32,4096]{2,1,0:T(8,128)(2,1)} %all-to-all-done.2), kind=kLoop, calls=%fused_computation | loop fusion | flops 8257536 | bytes 8912896 | tf_op jit(solution)/shard_map/reduce_sum | solution.py:68
  262.4 1.0 broadcast_in_dim.30
  263.4 106.4 %all_to_all.26 = bf16[32,32,4096]{2,1,0:T(8,128)(2,1)S(1)} all-to-all(bf16[32,32,4096]{2,1,0:T(8,128)(2,1)S(1)} %broadcast_in_dim.30), channel_id=1, replica_groups=mesh['dp'=32,'feat'=4] {'dp'}, dimensions={0} | all-to-all | bytes 16777216 | tf_op jit(solution)/shard_map/all_to_all | solution.py:11
  369.8 3.3 copy-done.2
  373.1 8.6 %convolution_convert_fusion.1 = bf16[768,4096]{1,0:T(8,128)(2,1)} fusion(bf16[1024,4096]{1,0:T(8,128)(2,1)S(1)} %bitcast.41, bf16[768,1024]{1,0:T(8,128)(2,1)S(1)} %copy-done.1, f32[1024]{0:T(1024)S(1)} %add_rsqrt_fusion, f32[1024]{0:T(1024)S(1)} %broadcast_multiply_fusion), kind=kOutput, calls=%fused_computation.2 | convolution fusion | flops 6448742400 | bytes 16261120 | tf_op jit(solution)/shard_map/dot_general | solution.py:80
  381.8 12.4 %fusion.14 = (f32[1024]{0:T(1024)S(1)}, f32[1024]{0:T(1024)S(1)}, f32[768,1024]{1,0:T(8,128)}) fusion(bf16[768,1024]{1,0:T(8,128)(2,1)S(1)} %copy-done.1, f32[1024]{0:T(1024)S(1)} %add_rsqrt_fusion, f32[1024]{0:T(1024)S(1)} %broadcast_multiply_fusion, bf16[768,4096]{1,0:T(8,128)(2,1)} %all-gather.3.cloned.1.call-done, bf16[1024,4096]{1,0:T(8,128)(2,1)} %bitcast.42), kind=kOutput, calls=%fused_computation.26 | convolution fusion | flops 6447167488 | bytes 19415040 | tf_op jit(solution)/shard_map/dot_general | solution.py:84
  394.1 46.9 %reduce-scatter.2.cloned.1.call-done = bf16[768,1024]{1,0:T(8,128)(2,1)} async-done(((bf16[768,4096]{1,0:T(8,128)(2,1)}), bf16[768,1024]{1,0:T(8,128)(2,1)}) %reduce-scatter.2.cloned.1.call-update) | async-done | bytes 1572880 | tf_op jit(solution)/shard_map/reduce_scatter | solution.py:81
  441.0 2.2 fusion.18
  444.0 23.8 %all_to_all.27 = f32[32,40,128]{2,1,0:T(8,128)} all-to-all(f32[32,40,128]{2,1,0:T(8,128)S(1)} %broadcast_in_dim.32), channel_id=1, replica_groups=mesh['dp'=32,'feat'=4] {'dp'}, dimensions={0} | all-to-all | bytes 1310720 | tf_op jit(solution)/shard_map/all_to_all | solution.py:11
  467.8 1.1 reduce_sum.198
  469.0 5.0 %all-gather = f32[4,1,128]{2,1,0:T(1,128)S(1)} all-gather(f32[1,1,128]{2,1,0:T(1,128)S(1)} %slice_bitcast_fusion), channel_id=1, replica_groups=mesh['dp'=32,'feat'=4] {'feat'}, dimensions={0}, use_global_device_ids=true | all-gather | bytes 2560 | tf_op jit(solution)/shard_map/all_gather | solution.py:97
  474.6 3.9 fusion.17
  478.6 2.0 fusion.7
  (38 shorter events, 4.0 us)
Async XLA Ops:
  7.2 3.7 copy-start.1
  7.2 94.0 %all-gather.3.cloned.1.call-start = ((), (), s32[]{:S(2)}) async-start(), calls=%async_computation.6 | async-start | bytes 7864320 | tf_op jit(solution)/shard_map/all_gather | solution.py:55
  10.9 29.2 %copy-start = (bf16[768,1024]{1,0:T(8,128)(2,1)S(1)}, bf16[768,1024]{1,0:T(8,128)(2,1)}, u32[]{:S(2)}) copy-start(bf16[768,1024]{1,0:T(8,128)(2,1)} %param.3) | copy-start | bytes 4718596
  42.8 70.2 %all-to-all-start.1 = ((f32[32,8,128]{2,1,0:T(8,128)}), f32[32,8,128]{2,1,0:T(8,128)S(1)}, u32[]{:S(2)}, u32[]{:S(2)}) async-start(f32[32,8,128]{2,1,0:T(8,128)} %broadcast_in_dim.27), calls=%async_computation.1 | async-start | bytes 262144 | tf_op jit(solution)/shard_map/all_to_all | solution.py:11
  113.0 143.3 %all-to-all-start.2 = ((bf16[32,32,4096]{2,1,0:T(8,128)(2,1)}), bf16[32,32,4096]{2,1,0:T(8,128)(2,1)}, u32[]{:S(2)}, u32[]{:S(2)}) async-start(bf16[32,32,4096]{2,1,0:T(8,128)(2,1)} %bitcast.40), calls=%async_computation.2 | async-start | bytes 16777216 | tf_op jit(solution)/shard_map/all_to_all | solution.py:11
  122.5 318.5 %reduce-scatter.2.cloned.1.call-start = ((), (), s32[]{:S(2)}) async-start(), calls=%async_computation.7 | async-start | bytes 7864320 | tf_op jit(solution)/shard_map/reduce_scatter | solution.py:81
  369.8 3.3 copy-start.2
  474.6 3.9 copy-start.3
Sparse Core Ops, SparseCore 0:
  42.3 58.8 all-gather.2
  381.9 59.1 reduce-scatter.1
